TPU v7x, 256 devices: a whole 4x4x8 slice. The times are simulated.
256 devices in a mesh: dp: 16 (over y, x), tensor: 16 (over z, core).
Axes of the slice: x: 4, y: 4, z: 8, core: 2. Of those that a mesh axis runs over, the one named last changes fastest.
Arguments:
- tokens: bfloat16 [4096, 6144], P('dp'), may hold values from -6 to 6
- target: bfloat16 [4096, 6144], P('dp'), may hold values from -6 to 6
- pair_bias: float32 [4096, 32, 256], P('dp', 'tensor'), may hold values from -6 to 680
- neighbours: int32 [4096, 256], P('dp'), may hold values 0 or 1
- w_query: bfloat16 [6144, 4096], P('dp', 'tensor'), may hold values from -0.078125 to 0.078125
- w_key: bfloat16 [6144, 4096], P('dp', 'tensor'), may hold values from -0.078125 to 0.078125
- w_value: bfloat16 [6144, 4096], P('dp', 'tensor'), may hold values from -0.078125 to 0.078125
- w_out: bfloat16 [4096, 6144], P('tensor', 'dp'), may hold values from -0.09375 to 0.09375
- basis_value: float32 [6144, 4096], P('dp', 'tensor'), may hold values from -32 to 32
- basis_out: float32 [4096, 6144], P('tensor', 'dp'), may hold values from -32 to 32
- prior_value: float32 [6144, 4096], P('dp', 'tensor'), may hold values from -32 to 32
- prior_out: float32 [4096, 6144], P('tensor', 'dp'), may hold values from -32 to 32
- prior_beta: float32 [], replicated, may hold values from 10 to 60
Outputs:
- next_value: float32 [6144, 4096], P('dp', 'tensor')
- next_out: float32 [4096, 6144], P('tensor', 'dp')
- coefficients: float32 [2], replicated
All inputs are finite; a program needn't handle non-finite values. No bound on the sum of `neighbours` on one device may be relied on, other than what follows from the above.
Results may differ from a plain program's by a relative error of at most 0.02.
Values may be sent and summed in bfloat16 or wider, within the bound.
A program may use at most 128 MiB of HBM per device.

v0:
```python
import math
import jax
import jax.numpy as jnp
from jax import lax
from jax.sharding import PartitionSpec as P

HEAD_DIM = 128
loss_gain = 32.0
epsilon = 1e-06


def body(
    tokens,
    target,
    pair_bias,
    neighbours,
    w_query,
    w_key,
    w_value,
    w_out,
    basis_value,
    basis_out,
    prior_value,
    prior_out,
    prior_beta,
):
    count = tokens.shape[0]
    features = tokens.shape[1]
    local_width = w_query.shape[1]
    heads_here = local_width // HEAD_DIM
    full_width = local_width * lax.axis_size("tensor")
    groups = lax.axis_size("dp")
    total_tokens = count * groups
    xf = tokens.astype(jnp.float32)
    normed = (xf * lax.rsqrt(jnp.mean(xf * xf, axis=1, keepdims=True) + epsilon)).astype(
        jnp.bfloat16
    )
    basis_value_b = basis_value.astype(jnp.bfloat16)
    pieces = (
        lax.all_gather(w_query, "dp", axis=0, tiled=True),
        lax.all_gather(w_key, "dp", axis=0, tiled=True),
        lax.all_gather(w_value, "dp", axis=0, tiled=True),
        lax.all_gather(basis_value_b, "dp", axis=0, tiled=True),
    )
    query_acc, key_acc, value_acc, tangent_acc = tuple(
        (jnp.dot(normed, piece, preferred_element_type=jnp.float32) for piece in pieces)
    )
    shape3 = (count, heads_here, HEAD_DIM)
    query = query_acc.astype(jnp.bfloat16).reshape(shape3)
    keys = key_acc.astype(jnp.bfloat16).reshape(shape3)
    values = value_acc.astype(jnp.bfloat16).reshape(shape3)
    tangent_values = (tangent_acc / math.sqrt(features)).astype(jnp.bfloat16).reshape(shape3)
    out_full, tangent_out = (
        lax.all_gather(w_out, "dp", axis=1, tiled=True),
        lax.all_gather(basis_out.astype(jnp.bfloat16), "dp", axis=1, tiled=True),
    )
    scores = (
        jnp.einsum("thd,shd->ths", query, keys, preferred_element_type=jnp.float32)
        / math.sqrt(HEAD_DIM)
        + pair_bias
    )
    rows = lax.broadcasted_iota(jnp.int32, (count, count), 0)
    cols = lax.broadcasted_iota(jnp.int32, (count, count), 1)
    allowed = (neighbours == 1) | (jnp.abs(rows - cols) <= 1)
    scores = jnp.where(allowed[:, None, :], scores, -jnp.inf)
    probs = jax.nn.softmax(scores, axis=2).astype(jnp.bfloat16)
    mixed = (
        jnp.einsum("ths,shd->thd", probs, values, preferred_element_type=jnp.float32)
        .astype(jnp.bfloat16)
        .reshape(count, local_width)
    )
    tangent_mixed = (
        jnp.einsum("ths,shd->thd", probs, tangent_values, preferred_element_type=jnp.float32)
        .astype(jnp.bfloat16)
        .reshape(count, local_width)
    )
    scale_out = 1.0 / math.sqrt(full_width)
    partial_value = jnp.dot(mixed, out_full, preferred_element_type=jnp.float32)
    tangent_partial = jnp.dot(
        mixed, tangent_out, preferred_element_type=jnp.float32
    ) * scale_out + jnp.dot(tangent_mixed, out_full, preferred_element_type=jnp.float32)
    attn, tangent_attn = (
        lax.psum(partial_value.astype(jnp.bfloat16), "tensor").astype(jnp.float32),
        lax.psum(tangent_partial.astype(jnp.bfloat16), "tensor").astype(jnp.float32),
    )
    factor = loss_gain * full_width / total_tokens
    error = ((xf + attn - target.astype(jnp.float32)) * factor).astype(jnp.bfloat16)
    tangent_error = (tangent_attn * factor).astype(jnp.bfloat16)
    first = jnp.einsum("td,ta->da", error, tangent_mixed, preferred_element_type=jnp.float32)
    second = jnp.einsum("td,ta->da", tangent_error, mixed, preferred_element_type=jnp.float32)
    curv_out = (
        lax.psum_scatter(
            ((first + second) * scale_out).astype(jnp.bfloat16),
            "dp",
            scatter_dimension=0,
            tiled=True,
        )
        .astype(jnp.float32)
        .T
    )
    back_tangent = (
        jnp.einsum("td,ad->ta", tangent_error, out_full, preferred_element_type=jnp.float32)
        + jnp.einsum("td,ad->ta", error, tangent_out, preferred_element_type=jnp.float32)
        * scale_out
    ).astype(jnp.bfloat16)
    value_back = (
        jnp.einsum(
            "ths,thd->shd", probs, back_tangent.reshape(shape3), preferred_element_type=jnp.float32
        )
        .astype(jnp.bfloat16)
        .reshape(count, local_width)
    )
    scale_value = 1.0 / math.sqrt(features)
    curv_value = lax.psum_scatter(
        (
            jnp.einsum("ti,ta->ia", normed, value_back, preferred_element_type=jnp.float32)
            * scale_value
        ).astype(jnp.bfloat16),
        "dp",
        scatter_dimension=0,
        tiled=True,
    ).astype(jnp.float32)
    entries = 2.0 * features * full_width
    alpha = (
        lax.psum(
            jnp.sum(basis_value * curv_value) + jnp.sum(basis_out * curv_out), ("dp", "tensor")
        )
        / entries
    )
    rest_value = curv_value - alpha * basis_value - prior_beta * prior_value
    rest_out = curv_out - alpha * basis_out - prior_beta * prior_out
    squares = (
        lax.psum(jnp.sum(rest_value * rest_value) + jnp.sum(rest_out * rest_out), ("dp", "tensor"))
        / entries
    )
    beta = jnp.sqrt(squares + epsilon)
    return (rest_value / beta, rest_out / beta, jnp.stack([alpha, beta]))


def solution(mesh):
    placed = (
        P("dp", None),
        P("dp", None),
        P("dp", "tensor", None),
        P("dp", None),
        P("dp", "tensor"),
        P("dp", "tensor"),
        P("dp", "tensor"),
        P("tensor", "dp"),
        P("dp", "tensor"),
        P("tensor", "dp"),
        P("dp", "tensor"),
        P("tensor", "dp"),
        P(),
    )
    return jax.shard_map(
        body,
        mesh=mesh,
        in_specs=placed,
        out_specs=(P("dp", "tensor"), P("tensor", "dp"), P()),
        check_vma=False,
    )
```

profile of v0, /device:TPU:1, one launch (start us, length us, event | category | flops | bytes accessed | tf_op | source)
XLA Modules:
  0.0 824.5 jit_solution(4294563663317649409)
XLA Ops:
  13.6 2.1 copy.19
  16.6 50.3 %all-gather.9.cloned.1.call-done = bf16[6144,256]{1,0:T(8,128)(2,1)} async-done(((bf16[384,256]{1,0:T(8,128)(2,1)}), bf16[6144,256]{1,0:T(8,128)(2,1)}) %all-gather.9.cloned.1.call-update) | async-done | bytes 3145744 | tf_op jit(solution)/shard_map/all_gather | solution.py:41
  66.9 3.4 convolution_convert_fusion.5
  70.4 51.0 %all-gather.11.cloned.1.call-done = bf16[6144,256]{1,0:T(8,128)(2,1)} async-done(((bf16[384,256]{1,0:T(8,128)(2,1)}), bf16[6144,256]{1,0:T(8,128)(2,1)}) %all-gather.11.cloned.1.call-update) | async-done | bytes 3145744 | tf_op jit(solution)/shard_map/all_gather | solution.py:40
  121.3 3.4 convolution_convert_fusion.4
  124.8 2.2 fusion.34
  128.1 47.7 %all-gather.7.cloned.1.call-done = bf16[6144,256]{1,0:T(8,128)(2,1)} async-done(((bf16[384,256]{1,0:T(8,128)(2,1)}), bf16[6144,256]{1,0:T(8,128)(2,1)}) %all-gather.7.cloned.1.call-update) | async-done | bytes 3145744 | tf_op jit(solution)/shard_map/all_gather | solution.py:42
  175.8 3.4 convolution_convert_fusion.6
  179.4 51.2 %all-gather.15.cloned.1.call-done = bf16[6144,256]{1,0:T(8,128)(2,1)} async-done(((bf16[384,256]{1,0:T(8,128)(2,1)}), bf16[6144,256]{1,0:T(8,128)(2,1)}) %all-gather.15.cloned.1.call-update) | async-done | bytes 3145744 | tf_op jit(solution)/shard_map/all_gather | solution.py:43
  230.6 3.4 fusion.18
  234.9 54.0 %all-gather.17.cloned.1.call-done = bf16[256,6144]{1,0:T(8,128)(2,1)} async-done(((bf16[256,384]{1,0:T(8,128)(2,1)}), bf16[256,6144]{1,0:T(8,128)(2,1)}) %all-gather.17.cloned.1.call-update) | async-done | bytes 3145744 | tf_op jit(solution)/shard_map/all_gather | solution.py:54
  288.9 4.5 convolution_convert_fusion
  293.4 55.4 %all-gather.13.cloned.1.call-done = bf16[256,6144]{1,0:T(8,128)(2,1)} async-done(((bf16[256,384]{1,0:T(8,128)(2,1)}), bf16[256,6144]{1,0:T(8,128)(2,1)}) %all-gather.13.cloned.1.call-update) | async-done | bytes 3145744 | tf_op jit(solution)/shard_map/all_gather | solution.py:55
  348.8 3.0 convolution_multiply_fusion.1
  351.9 2.7 fusion.3
  354.8 127.6 %all-reduce.3.cloned.1.call-done = (bf16[256,6144]{1,0:T(8,128)(2,1)}, bf16[256,6144]{1,0:T(8,128)(2,1)}) async-done(((bf16[256,6144]{1,0:T(8,128)(2,1)}, bf16[256,6144]{1,0:T(8,128)(2,1)}), (bf16[256,6144]{1,0:T(8,128)(2,1)}, bf16[256,6144]{1,0:T(8,128)(2,1)})) %all-reduce.3.cloned.1.call-update) | async-done | bytes 6291472 | tf_op jit(solution)/shard_map/psum | solution.py:83
  482.4 5.5 convolution_multiply_fusion.3
  489.2 3.0 fusion.4
  493.1 5.5 fusion.26
  498.6 3.3 fusion.2
  503.7 68.5 %reduce-scatter.3.cloned.1.call-done = bf16[384,256]{1,0:T(8,128)(2,1)} async-done(((bf16[6144,256]{1,0:T(8,128)(2,1)}), bf16[384,256]{1,0:T(8,128)(2,1)}) %reduce-scatter.3.cloned.1.call-update) | async-done | bytes 196624 | tf_op jit(solution)/shard_map/reduce_scatter | solution.py:114
  573.9 82.0 %reduce-scatter.5.cloned.1.call-done = bf16[384,256]{1,0:T(8,128)(2,1)} async-done(((bf16[6144,256]{1,0:T(8,128)(2,1)}), bf16[384,256]{1,0:T(8,128)(2,1)}) %reduce-scatter.5.cloned.1.call-update) | async-done | bytes 196624 | tf_op jit(solution)/shard_map/reduce_scatter | solution.py:92
  659.1 77.2 %psum.30 = f32[]{:T(128)} all-reduce(f32[]{:T(128)S(6)} %add.54), channel_id=1, replica_groups=mesh['dp'=16,'tensor'=16] {'dp','tensor'}, use_global_device_ids=true, to_apply=%region_9.10 | all-reduce | flops 1 | bytes 8 | tf_op jit(solution)/shard_map/psum | solution.py:125
  741.5 73.3 %psum.31 = f32[]{:T(128)} all-reduce(f32[]{:T(128)S(6)} %add.55), channel_id=1, replica_groups=mesh['dp'=16,'tensor'=16] {'dp','tensor'}, use_global_device_ids=true, to_apply=%region_12.13 | all-reduce | flops 1 | bytes 8 | tf_op jit(solution)/shard_map/psum | solution.py:133
  (67 shorter events, 22.2 us)
Async XLA Ops:
  7.2 8.5 %copy-start.13 = (s32[256,256]{1,0:T(8,128)S(1)}, s32[256,256]{1,0:T(8,128)}, u32[]{:S(2)}) copy-start(s32[256,256]{1,0:T(8,128)} %param.16) | copy-start | bytes 786436
  7.2 8.7 %copy-start = (bf16[256,6144]{1,0:T(8,128)(2,1)S(1)}, bf16[256,6144]{1,0:T(8,128)(2,1)}, u32[]{:S(2)}) copy-start(bf16[256,6144]{1,0:T(8,128)(2,1)} %param.13) | copy-start | bytes 9437188
  7.2 59.8 %all-gather.9.cloned.1.call-start = ((), (), s32[]{:S(2)}) async-start(), calls=%async_computation.3 | async-start | bytes 3342336 | tf_op jit(solution)/shard_map/all_gather | solution.py:41
  7.9 113.4 %all-gather.11.cloned.1.call-start = ((), (), s32[]{:S(2)}) async-start(), calls=%async_computation.4 | async-start | bytes 3342336 | tf_op jit(solution)/shard_map/all_gather | solution.py:40
  8.7 167.1 %all-gather.7.cloned.1.call-start = ((), (), s32[]{:S(2)}) async-start(), calls=%async_computation.2 | async-start | bytes 3342336 | tf_op jit(solution)/shard_map/all_gather | solution.py:42
  9.4 221.2 %all-gather.15.cloned.1.call-start = ((), (), s32[]{:S(2)}) async-start(), calls=%async_computation.6 | async-start | bytes 3342336 | tf_op jit(solution)/shard_map/all_gather | solution.py:43
  11.2 277.7 %all-gather.17.cloned.1.call-start = ((), (), s32[]{:S(2)}) async-start(), calls=%async_computation.7 | async-start | bytes 3342336 | tf_op jit(solution)/shard_map/all_gather | solution.py:54
  11.8 337.0 %all-gather.13.cloned.1.call-start = ((), (), s32[]{:S(2)}) async-start(), calls=%async_computation.5 | async-start | bytes 3342336 | tf_op jit(solution)/shard_map/all_gather | solution.py:55
  13.5 468.8 %all-reduce.3.cloned.1.call-start = ((), (), s32[]{:S(2)}) async-start(), calls=%async_computation.10 | async-start | bytes 12582912 | tf_op jit(solution)/shard_map/psum | solution.py:83
  348.8 3.1 copy-start.1
  348.8 3.1 copy-start.10
  354.6 217.6 %reduce-scatter.3.cloned.1.call-start = ((), (), s32[]{:S(2)}) async-start(), calls=%async_computation.8 | async-start | bytes 3342336 | tf_op jit(solution)/shard_map/reduce_scatter | solution.py:114
  482.4 5.5 copy-start.2
  482.4 5.6 copy-start.4
  492.2 0.9 copy-start.11
  492.2 163.7 %reduce-scatter.5.cloned.1.call-start = ((), (), s32[]{:S(2)}) async-start(), calls=%async_computation.9 | async-start | bytes 3342336 | tf_op jit(solution)/shard_map/reduce_scatter | solution.py:92
  493.1 5.5 copy-start.5
  501.9 1.0 copy-start.8
  501.9 70.3 %copy-start.3 = (f32[384,256]{1,0:T(8,128)S(1)}, f32[384,256]{1,0:T(8,128)}, u32[]{:S(2)}) copy-start(f32[384,256]{1,0:T(8,128)} %param.21) | copy-start | bytes 1179652
  501.9 157.0 %copy-start.12 = (f32[256,384]{1,0:T(8,128)S(1)}, f32[256,384]{1,0:T(8,128)}, u32[]{:S(2)}) copy-start(f32[256,384]{1,0:T(8,128)} %param.24) | copy-start | bytes 1179652
  501.9 235.1 %copy-start.9 = (f32[384,256]{1,0:T(8,128)S(1)}, f32[384,256]{1,0:T(8,128)}, u32[]{:S(2)}) copy-start(f32[384,256]{1,0:T(8,128)} %param.23) | copy-start | bytes 1179652
  572.2 245.0 %copy-start.6 = (bf16[384,256]{1,0:T(8,128)(2,1)S(1)}, bf16[384,256]{1,0:T(8,128)(2,1)}, u32[]{:S(2)}) copy-start(bf16[384,256]{1,0:T(8,128)(2,1)} %reduce-scatter.3.cloned.1.call-done) | copy-start | bytes 589828
  655.9 159.6 %copy-start.7 = (bf16[384,256]{1,0:T(8,128)(2,1)S(1)}, bf16[384,256]{1,0:T(8,128)(2,1)}, u32[]{:S(2)}) copy-start(bf16[384,256]{1,0:T(8,128)(2,1)} %reduce-scatter.5.cloned.1.call-done) | copy-start | bytes 589828
Sparse Core Ops, SparseCore 0:
  10.4 56.4 all-gather.8
  69.4 51.9 all-gather.10
  123.8 51.9 all-gather.6
  178.6 51.9 all-gather.14
  232.8 56.0 all-gather.16
  291.7 57.0 all-gather.12
  354.7 127.6 all-reduce.2
  492.3 79.7 reduce-scatter.2
  575.8 80.0 reduce-scatter.4
where the time goes:
time: 825 us; the launch traced here: 824 us
  waiting for transfers between devices  590 us (72%)
  blocking collectives  150 us (18%)
  matrix products  45.7 us (6%)
  between operations  18.6 us (2%)
  other arithmetic  13.4 us (2%)
    psum x1, waiting for transfers between devices, body(): lax.psum(partial_value.astype(jnp.bfloat16), 'tensor').astype(jnp.float32)  128 us
    reduce_scatter x1, waiting for transfers between devices, body(): lax.psum_scatter(((first + second) * scale_out).astype(jnp.bfloat16), 'dp...  82 us
    psum x1, blocking collectives, body(): lax.psum(jnp.sum(basis_value * curv_value) + jnp.sum(basis_out * curv_out...  77.2 us
    psum x1, blocking collectives, body(): lax.psum(jnp.sum(rest_value * rest_value) + jnp.sum(rest_out * rest_out),...  73.3 us
    reduce_scatter x1, waiting for transfers between devices, body(): lax.psum_scatter((jnp.einsum('ti,ta->ia', normed, value_back, preferred_e...  68.5 us
    all_gather x1, waiting for transfers between devices, body(): lax.all_gather(basis_out.astype(jnp.bfloat16), 'dp', axis=1, tiled=True)  55.4 us
    all_gather x1, waiting for transfers between devices, body(): lax.all_gather(w_out, 'dp', axis=1, tiled=True)  54 us
    all_gather x1, waiting for transfers between devices, body(): lax.all_gather(basis_value_b, 'dp', axis=0, tiled=True)  51.2 us
  transfers between devices with their start and end apart: 9, of which 9 were waited for; matrix products, arithmetic and copies ran while one was open for 5% of the time, Pallas kernels for 0%

commit v1 on v0

--- a/solution.py
+++ b/solution.py
@@ -80,7 +80,9 @@
         mixed, tangent_out, preferred_element_type=jnp.float32
     ) * scale_out + jnp.dot(tangent_mixed, out_full, preferred_element_type=jnp.float32)
     attn, tangent_attn = (
-        lax.psum(partial_value.astype(jnp.bfloat16), "tensor").astype(jnp.float32),
+        jnp.sum(lax.all_gather(partial_value.astype(jnp.bfloat16), "tensor"), axis=0).astype(
+            jnp.float32
+        ),
         lax.psum(tangent_partial.astype(jnp.bfloat16), "tensor").astype(jnp.float32),
     )
     factor = loss_gain * full_width / total_tokens

time: 825 us -> 1060 us (1.28)
  waiting for transfers between devices: 590 us -> 806 us
  other arithmetic: 13.4 us -> 32.1 us
    all_gather x0 -> x1, waiting for transfers between devices: none -> 250 us  [body(): lax.all_gather(partial_value.astype(jnp.bfloat16), 'tensor')]
    psum x1, waiting for transfers between devices: 128 us -> 93.5 us  [body(): lax.psum(tangent_partial.astype(jnp.bfloat16), 'tensor').astype(jnp.float32)]
    reduce_sum x0 -> x1, other arithmetic: none -> 18.7 us  [body(): jnp.sum(lax.all_gather(partial_value.astype(jnp.bfloat16), 'tensor'), axi...]
  transfers between devices with their start and end apart: 9 -> 10, of which waited for: 9 -> 10; matrix products, arithmetic and copies ran while one was open for 5% -> 7% of each run, Pallas kernels for 0% -> 0%
where the time goes in v1:
time: 1060 us
  waiting for transfers between devices  806 us (76%)
  blocking collectives  151 us (14%)
  matrix products  49.1 us (5%)
  other arithmetic  32.1 us (3%)
  between operations  19 us (2%)
    all_gather x1, waiting for transfers between devices, body(): lax.all_gather(partial_value.astype(jnp.bfloat16), 'tensor')  250 us
    psum x1, waiting for transfers between devices, body(): lax.psum(tangent_partial.astype(jnp.bfloat16), 'tensor').astype(jnp.float32)  93.5 us
    reduce_scatter x1, waiting for transfers between devices, body(): lax.psum_scatter(((first + second) * scale_out).astype(jnp.bfloat16), 'dp...  82 us
    psum x1, blocking collectives, body(): lax.psum(jnp.sum(basis_value * curv_value) + jnp.sum(basis_out * curv_out...  77.2 us
    psum x1, blocking collectives, body(): lax.psum(jnp.sum(rest_value * rest_value) + jnp.sum(rest_out * rest_out),...  73.4 us
    reduce_scatter x1, waiting for transfers between devices, body(): lax.psum_scatter((jnp.einsum('ti,ta->ia', normed, value_back, preferred_e...  68.4 us
    all_gather x1, waiting for transfers between devices, body(): lax.all_gather(w_out, 'dp', axis=1, tiled=True)  54.7 us
    all_gather x1, waiting for transfers between devices, body(): lax.all_gather(basis_out.astype(jnp.bfloat16), 'dp', axis=1, tiled=True)  54.6 us
  transfers between devices with their start and end apart: 10, of which 10 were waited for; matrix products, arithmetic and copies ran while one was open for 7% of the time, Pallas kernels for 0%

profile of v1, /device:TPU:1, one launch (start us, length us, event | category | flops | bytes accessed | tf_op | source)
XLA Modules:
  0.0 1062.8 jit_solution(3429953072142666800)
XLA Ops:
  16.6 50.4 %all-gather.11.cloned.1.call-done = bf16[6144,256]{1,0:T(8,128)(2,1)} async-done(((bf16[384,256]{1,0:T(8,128)(2,1)}), bf16[6144,256]{1,0:T(8,128)(2,1)}) %all-gather.11.cloned.1.call-update) | async-done | bytes 3145744 | tf_op jit(solution)/shard_map/all_gather | solution.py:41
  66.9 3.4 convolution_convert_fusion.5
  70.4 51.0 %all-gather.13.cloned.1.call-done = bf16[6144,256]{1,0:T(8,128)(2,1)} async-done(((bf16[384,256]{1,0:T(8,128)(2,1)}), bf16[6144,256]{1,0:T(8,128)(2,1)}) %all-gather.13.cloned.1.call-update) | async-done | bytes 3145744 | tf_op jit(solution)/shard_map/all_gather | solution.py:40
  121.3 3.4 convolution_convert_fusion.4
  128.0 47.7 %all-gather.9.cloned.1.call-done = bf16[6144,256]{1,0:T(8,128)(2,1)} async-done(((bf16[384,256]{1,0:T(8,128)(2,1)}), bf16[6144,256]{1,0:T(8,128)(2,1)}) %all-gather.9.cloned.1.call-update) | async-done | bytes 3145744 | tf_op jit(solution)/shard_map/all_gather | solution.py:42
  175.8 3.4 convolution_convert_fusion.6
  179.4 54.7 %all-gather.19.cloned.1.call-done = bf16[256,6144]{1,0:T(8,128)(2,1)} async-done(((bf16[256,384]{1,0:T(8,128)(2,1)}), bf16[256,6144]{1,0:T(8,128)(2,1)}) %all-gather.19.cloned.1.call-update) | async-done | bytes 3145744 | tf_op jit(solution)/shard_map/all_gather | solution.py:54
  234.0 4.5 convolution_convert_fusion
  238.6 51.3 %all-gather.17.cloned.1.call-done = bf16[6144,256]{1,0:T(8,128)(2,1)} async-done(((bf16[384,256]{1,0:T(8,128)(2,1)}), bf16[6144,256]{1,0:T(8,128)(2,1)}) %all-gather.17.cloned.1.call-update) | async-done | bytes 3145744 | tf_op jit(solution)/shard_map/all_gather | solution.py:43
  289.9 3.4 fusion.18
  294.2 54.6 %all-gather.15.cloned.1.call-done = bf16[256,6144]{1,0:T(8,128)(2,1)} async-done(((bf16[256,384]{1,0:T(8,128)(2,1)}), bf16[256,6144]{1,0:T(8,128)(2,1)}) %all-gather.15.cloned.1.call-update) | async-done | bytes 3145744 | tf_op jit(solution)/shard_map/all_gather | solution.py:55
  348.8 3.0 convolution_multiply_fusion.1
  354.8 250.0 %all-gather.21.cloned.1.call-done = bf16[4096,6144]{1,0:T(8,128)(2,1)} async-done(((bf16[256,6144]{1,0:T(8,128)(2,1)}), bf16[4096,6144]{1,0:T(8,128)(2,1)}) %all-gather.21.cloned.1.call-update) | async-done | bytes 50331664 | tf_op jit(solution)/shard_map/all_gather | solution.py:83
  604.8 18.7 %reduce_sum.68 = bf16[256,6144]{1,0:T(8,128)(2,1)} reduce(bf16[16,256,6144]{2,1,0:T(8,128)(2,1)} %bitcast.59, bf16[]{:T(256)} %constant.30.clone.1), dimensions={0}, to_apply=%region_4.5 | reduce | flops 23592960 | bytes 53477376 | tf_op jit(solution)/shard_map/reduce_sum | solution.py:83
  623.5 6.2 convolution_multiply_fusion.3
  629.6 93.5 %all-reduce.2.cloned.1.call-done = bf16[256,6144]{1,0:T(8,128)(2,1)} async-done(((bf16[256,6144]{1,0:T(8,128)(2,1)}), bf16[256,6144]{1,0:T(8,128)(2,1)}) %all-reduce.2.cloned.1.call-update) | async-done | bytes 3145744 | tf_op jit(solution)/shard_map/psum | solution.py:86
  723.2 3.9 fusion.17
  727.3 3.0 fusion.4
  731.1 5.5 fusion.26
  736.7 3.2 fusion.2
  741.7 68.4 %reduce-scatter.3.cloned.1.call-done = bf16[384,256]{1,0:T(8,128)(2,1)} async-done(((bf16[6144,256]{1,0:T(8,128)(2,1)}), bf16[384,256]{1,0:T(8,128)(2,1)}) %reduce-scatter.3.cloned.1.call-update) | async-done | bytes 196624 | tf_op jit(solution)/shard_map/reduce_scatter | solution.py:116
  811.8 82.0 %reduce-scatter.5.cloned.1.call-done = bf16[384,256]{1,0:T(8,128)(2,1)} async-done(((bf16[6144,256]{1,0:T(8,128)(2,1)}), bf16[384,256]{1,0:T(8,128)(2,1)}) %reduce-scatter.5.cloned.1.call-update) | async-done | bytes 196624 | tf_op jit(solution)/shard_map/reduce_scatter | solution.py:94
  897.0 77.2 %psum.22 = f32[]{:T(128)} all-reduce(f32[]{:T(128)S(6)} %add.52), channel_id=1, replica_groups=mesh['dp'=16,'tensor'=16] {'dp','tensor'}, use_global_device_ids=true, to_apply=%region_9.10 | all-reduce | flops 1 | bytes 8 | tf_op jit(solution)/shard_map/psum | solution.py:127
  979.4 73.4 %psum.23 = f32[]{:T(128)} all-reduce(f32[]{:T(128)S(6)} %add.53), channel_id=1, replica_groups=mesh['dp'=16,'tensor'=16] {'dp','tensor'}, use_global_device_ids=true, to_apply=%region_12.13 | all-reduce | flops 1 | bytes 8 | tf_op jit(solution)/shard_map/psum | solution.py:135
  (67 shorter events, 28.1 us)
Async XLA Ops:
  7.2 8.4 copy-start.11
  7.2 8.7 copy-start
  7.2 59.8 %all-gather.11.cloned.1.call-start = ((), (), s32[]{:S(2)}) async-start(), calls=%async_computation.3 | async-start | bytes 3342336 | tf_op jit(solution)/shard_map/all_gather | solution.py:41
  7.9 113.4 %all-gather.13.cloned.1.call-start = ((), (), s32[]{:S(2)}) async-start(), calls=%async_computation.4 | async-start | bytes 3342336 | tf_op jit(solution)/shard_map/all_gather | solution.py:40
  8.7 167.1 %all-gather.9.cloned.1.call-start = ((), (), s32[]{:S(2)}) async-start(), calls=%async_computation.2 | async-start | bytes 3342336 | tf_op jit(solution)/shard_map/all_gather | solution.py:42
  9.4 224.6 %all-gather.19.cloned.1.call-start = ((), (), s32[]{:S(2)}) async-start(), calls=%async_computation.7 | async-start | bytes 3342336 | tf_op jit(solution)/shard_map/all_gather | solution.py:54
  10.0 279.9 %all-gather.17.cloned.1.call-start = ((), (), s32[]{:S(2)}) async-start(), calls=%async_computation.6 | async-start | bytes 3342336 | tf_op jit(solution)/shard_map/all_gather | solution.py:43
  11.7 337.0 %all-gather.15.cloned.1.call-start = ((), (), s32[]{:S(2)}) async-start(), calls=%async_computation.5 | async-start | bytes 3342336 | tf_op jit(solution)/shard_map/all_gather | solution.py:55
  13.5 591.3 %all-gather.21.cloned.1.call-start = ((), (), s32[]{:S(2)}) async-start(), calls=%async_computation.11 | async-start | bytes 53477376 | tf_op jit(solution)/shard_map/all_gather | solution.py:83
  238.6 484.6 %all-reduce.2.cloned.1.call-start = ((), (), s32[]{:S(2)}) async-start(), calls=%async_computation.8 | async-start | bytes 6291456 | tf_op jit(solution)/shard_map/psum | solution.py:86
  348.8 3.1 copy-start.1
  348.8 3.1 copy-start.8
  354.5 455.6 %reduce-scatter.3.cloned.1.call-start = ((), (), s32[]{:S(2)}) async-start(), calls=%async_computation.9 | async-start | bytes 3342336 | tf_op jit(solution)/shard_map/reduce_scatter | solution.py:116
  730.2 0.9 copy-start.9
  730.3 163.6 %reduce-scatter.5.cloned.1.call-start = ((), (), s32[]{:S(2)}) async-start(), calls=%async_computation.10 | async-start | bytes 3342336 | tf_op jit(solution)/shard_map/reduce_scatter | solution.py:94
  731.1 5.5 copy-start.3
  739.9 1.0 copy-start.6
  739.9 70.2 %copy-start.2 = (f32[384,256]{1,0:T(8,128)S(1)}, f32[384,256]{1,0:T(8,128)}, u32[]{:S(2)}) copy-start(f32[384,256]{1,0:T(8,128)} %param.21) | copy-start | bytes 1179652
  739.9 156.9 %copy-start.10 = (f32[256,384]{1,0:T(8,128)S(1)}, f32[256,384]{1,0:T(8,128)}, u32[]{:S(2)}) copy-start(f32[256,384]{1,0:T(8,128)} %param.24) | copy-start | bytes 1179652
  739.9 234.9 %copy-start.7 = (f32[384,256]{1,0:T(8,128)S(1)}, f32[384,256]{1,0:T(8,128)}, u32[]{:S(2)}) copy-start(f32[384,256]{1,0:T(8,128)} %param.23) | copy-start | bytes 1179652
  810.1 245.0 %copy-start.4 = (bf16[384,256]{1,0:T(8,128)(2,1)S(1)}, bf16[384,256]{1,0:T(8,128)(2,1)}, u32[]{:S(2)}) copy-start(bf16[384,256]{1,0:T(8,128)(2,1)} %reduce-scatter.3.cloned.1.call-done) | copy-start | bytes 589828
  893.8 159.7 %copy-start.5 = (bf16[384,256]{1,0:T(8,128)(2,1)S(1)}, bf16[384,256]{1,0:T(8,128)(2,1)}, u32[]{:S(2)}) copy-start(bf16[384,256]{1,0:T(8,128)(2,1)} %reduce-scatter.5.cloned.1.call-done) | copy-start | bytes 589828
Sparse Core Ops, SparseCore 0:
  10.4 56.4 all-gather.10
  69.4 51.9 all-gather.12
  123.8 51.9 all-gather.8
  178.0 55.9 all-gather.18
  236.9 52.9 all-gather.16
  292.7 55.9 all-gather.14
  350.6 254.1 all-gather.20
  607.2 115.9 all-reduce.1
  730.4 79.6 reduce-scatter.2
  813.6 80.1 reduce-scatter.4
